TPU v7x, 256 devices: a whole 4x4x8 slice. The times are simulated.
256 devices in a mesh: rows: 8 (over z), hidden: 32 (over x, y, core).
Axes of the slice: x: 4, y: 4, z: 8, core: 2. Of those that a mesh axis runs over, the one named last changes fastest.
Arguments:
- tokens: bfloat16 [1024, 8192], P('hidden', 'rows'), may hold values from -6 to 6
- snapshot: int32 [1024, 1], replicated, may hold values from 0 to 63; in each aligned block of 1024 rows (0 to 1023, 1024 to 2047, ...) at most 32 rows name the same one
- gate_weight: bfloat16 [8192, 28672], P('rows', 'hidden'), may hold values from -0.0625 to 0.0625
- up_weight: bfloat16 [8192, 28672], P('rows', 'hidden'), may hold values from -0.0625 to 0.0625
- down_weight: bfloat16 [28672, 8192], P('hidden', 'rows'), may hold values from -0.03125 to 0.03125
- adapter_input_maps: bfloat16 [64, 8192, 128], P('hidden', 'rows')
- adapter_middle_maps: bfloat16 [64, 2, 64, 28672], P(None, None, 'rows', 'hidden'), may hold values from -0.375 to 0.375
- down_input_map: bfloat16 [64, 64, 28672], P(None, 'rows', 'hidden')
- down_output_map: bfloat16 [64, 64, 8192], P('hidden', None, 'rows'), may hold values from -0.75 to 0.75
Outputs:
- mixed: bfloat16 [1024, 8192], P('hidden', 'rows')
Inputs may be any that keep to these rules, and one draw needn't show every extreme that they name: Every snapshot is named by at least one row and by at most 32 rows; some snapshot is named by exactly 32 rows.
All inputs are finite; a program needn't handle non-finite values.
Results may differ from a plain program's by a relative error of at most 0.033.
Values may be sent and summed in bfloat16 or wider, within the bound.
No kernel may reach another device: no remote copies, remote signals or barrier semaphores. Data moves between devices by JAX's collectives and lax.ppermute only.
A program may use at most 128 MiB of HBM per device.

v0:
```python
import jax
import jax.numpy as jnp
from jax import lax
from jax.sharding import PartitionSpec as P


def slot_tables(snapshot, snapshot_total, capacity):
    row_total = snapshot.shape[0]
    snap_owner = snapshot[:, 0]
    onehot = (snap_owner[:, None] == jnp.arange(snapshot_total, dtype=jnp.int32)[None, :]).astype(
        jnp.int32
    )
    before = jnp.cumsum(onehot, axis=0) - onehot
    slot_index = jnp.sum(before * onehot, axis=1)
    token_of = jnp.full((snapshot_total, capacity), row_total, jnp.int32)
    token_of = token_of.at[snap_owner, slot_index].set(jnp.arange(row_total, dtype=jnp.int32))
    return (snap_owner, slot_index, token_of)


def swiglu(paired):
    return (jax.nn.silu(paired[:, 0]) * paired[:, 1]).astype(jnp.bfloat16)


def per_device(
    tokens,
    snapshot,
    gate_weight,
    up_weight,
    down_weight,
    adapter_input_maps,
    adapter_middle_maps,
    down_input_map,
    down_output_map,
):
    row_index = lax.axis_index("rows")
    hidden_index = lax.axis_index("hidden")
    all_count = snapshot.shape[0]
    snapshot_total = adapter_middle_maps.shape[0]
    capacity = 2 * all_count // snapshot_total
    snapshot_local = adapter_input_maps.shape[0]
    rank_block_values = adapter_middle_maps.shape[2]
    rank_full = down_output_map.shape[1]
    snap_owner, slot_index, token_of = slot_tables(snapshot, snapshot_total, capacity)
    filled_flag = token_of < all_count
    clamped_index = jnp.minimum(token_of, all_count - 1)
    own_first = hidden_index * snapshot_local
    own_clamped = lax.dynamic_slice_in_dim(clamped_index, own_first, snapshot_local, 0)
    own_filled = lax.dynamic_slice_in_dim(filled_flag, own_first, snapshot_local, 0)
    own_tokens = lax.dynamic_slice_in_dim(token_of, own_first, snapshot_local, 0)
    gathered = lax.all_gather(tokens, "hidden", axis=0, tiled=True)
    picked_snapshot = jnp.where(
        own_filled[:, :, None], gathered[own_clamped], jnp.zeros((), gathered.dtype)
    )
    rank_partial_values = jnp.einsum(
        "leh,lhr->ler", picked_snapshot, adapter_input_maps, preferred_element_type=jnp.float32
    )
    rank_partial_values = rank_partial_values.reshape(snapshot_local, capacity, 2, rank_full)
    placed = jnp.zeros((snapshot_total, capacity, 2, rank_full), jnp.float32)
    placed = lax.dynamic_update_slice_in_dim(placed, rank_partial_values, own_first, 0)
    rank_total = lax.psum(placed, ("rows", "hidden"))
    rank_activation_values = lax.dynamic_slice_in_dim(
        rank_total, row_index * rank_block_values, rank_block_values, 3
    ).astype(jnp.bfloat16)
    halves = []
    for half_position in range(2):
        grouped_rows = jnp.einsum(
            "sck,skf->scf",
            rank_activation_values[:, :, half_position],
            adapter_middle_maps[:, half_position],
            preferred_element_type=jnp.float32,
        )
        halves.append(grouped_rows[snap_owner, slot_index])
    adapter_gate_up = jnp.stack(halves, axis=1)
    gate_term = jnp.dot(gathered, gate_weight, preferred_element_type=jnp.float32)
    up_term = jnp.dot(gathered, up_weight, preferred_element_type=jnp.float32)
    adapter_rows = adapter_gate_up
    summed = lax.psum(
        (jnp.stack([gate_term, up_term], axis=1) + adapter_rows).astype(jnp.bfloat16), "rows"
    ).astype(jnp.float32)
    hidden_all = swiglu(summed)
    rows_grouped = jnp.where(
        filled_flag[:, :, None], hidden_all[clamped_index], jnp.zeros((), hidden_all.dtype)
    )
    down_part = jnp.einsum(
        "scf,skf->sck", rows_grouped, down_input_map, preferred_element_type=jnp.float32
    )
    placed_down = jnp.zeros((snapshot_total, capacity, rank_full), jnp.float32)
    placed_down = lax.dynamic_update_slice_in_dim(
        placed_down, down_part, row_index * rank_block_values, 2
    )
    down_total = lax.psum(placed_down, ("rows", "hidden"))
    down_rank = lax.dynamic_slice_in_dim(down_total, own_first, snapshot_local, 0).astype(
        jnp.bfloat16
    )
    lifted = jnp.einsum(
        "sck,skd->scd", down_rank, down_output_map, preferred_element_type=jnp.float32
    )
    feature_width = lifted.shape[2]
    adapter_down = jnp.zeros((all_count + 1, feature_width), jnp.float32)
    adapter_down = adapter_down.at[own_tokens.reshape(-1)].add(lifted.reshape(-1, feature_width))[
        :all_count
    ]
    adapter_rows = adapter_down
    return lax.psum_scatter(
        (
            jnp.dot(hidden_all, down_weight, preferred_element_type=jnp.float32) + adapter_rows
        ).astype(jnp.bfloat16),
        "hidden",
        scatter_dimension=0,
        tiled=True,
    )


def solution(mesh):
    return jax.shard_map(
        per_device,
        mesh=mesh,
        in_specs=(
            P("hidden", "rows"),
            P(),
            P("rows", "hidden"),
            P("rows", "hidden"),
            P("hidden", "rows"),
            P("hidden", "rows", None),
            P(None, None, "rows", "hidden"),
            P(None, "rows", "hidden"),
            P("hidden", None, "rows"),
        ),
        out_specs=P("hidden", "rows"),
        check_vma=False,
    )
```

profile of v0, /device:TPU:2, one launch (start us, length us, event | category | flops | bytes accessed | tf_op | source)
XLA Modules:
  0.0 571.1 jit_solution(12695949925899009694)
XLA Ops:
  6.5 0.0 copy-start
  6.5 0.0 all-gather.2.cloned.1.call-start
  6.5 0.7 all-gather.2.cloned.1.call-update
  7.3 0.0 all-reduce.4.cloned.1.call-start
  7.3 0.7 fusion.19
  8.0 18.0 %reduce-window.6 = s32[64,8,128]{2,1,0:T(8,128)S(1)} reduce-window(s32[64,8,128]{2,1,0:T(8,128)S(1)} %fusion.19, s32[]{:T(128)} %constant.16.clone.1), window={size=1x1x128 pad=0_0x0_0x127_0}, to_apply=%region_0.0 | reduce-window | flops 8323072 | bytes 524292 | tf_op jit(solution)/shard_map/reduce-window
  26.0 0.1 slice.44
  26.2 0.1 copy.13
  26.4 0.1 copy.14
  26.4 0.1 broadcast_add_fusion
  26.6 0.8 fusion.18
  27.3 0.7 shift-left_or_fusion
  28.1 0.7 multiply_reduce_fusion
  28.8 0.8 and_reduce_fusion
  29.6 4.3 scatter_custom_fusion.1
  33.9 0.1 reshape.74
  34.0 0.1 compare_select_fusion.1
  34.1 0.1 copy.16
  34.1 0.1 reshape.78
  34.2 0.1 dynamic-slice_bitcast_fusion.1
  34.3 0.1 copy.15
  34.4 26.9 %all-gather.2.cloned.1.call-done = bf16[1024,1024]{1,0:T(8,128)(2,1)} async-done(((bf16[32,1024]{1,0:T(8,128)(2,1)}), bf16[1024,1024]{1,0:T(8,128)(2,1)}) %all-gather.2.cloned.1.call-update) | async-done | bytes 2097168 | tf_op jit(solution)/shard_map/all_gather | solution.py:50
  61.4 2.7 gather_fusion
  64.0 0.0 copy-done.5
  64.0 0.3 fusion.20
  64.3 0.1 reshape.69
  64.4 0.1 copy.17
  64.5 2.5 broadcast_in_dim.49
  67.0 0.6 constant_dynamic-update-slice_fusion
  67.6 130.6 %all-reduce.5 = bf16[64,32,2,64]{1,3,0,2:T(8,128)(2,1)} all-reduce(f32[64,32,2,64]{1,3,0,2:T(8,128)} %constant_dynamic-update-slice_fusion), channel_id=1, replica_groups=mesh['rows'=8,'hidden'=32] {'rows','hidden'}, use_global_device_ids=true, to_apply=%region_4.5 | all-reduce | flops 262144 | bytes 1572864 | tf_op jit(solution)/shard_map/psum | solution.py:60
  198.2 1.0 dynamic-slice_convert_fusion
  199.2 0.0 copy-start.3
  199.2 5.5 fusion.12
  204.7 0.0 copy-done.3
  204.7 4.1 fusion.10
  208.8 19.8 %gather_fusion.1 = f32[1024,896]{1,0:T(8,128)} fusion(f32[64,32,896]{2,1,0:T(8,128)} %fusion.12, s32[1024]{0:T(1024)S(1)} %bitcast.78), kind=kCustom, calls=%fused_computation.1 | custom fusion | bytes 7348224 | tf_op jit(solution)/shard_map/gather | solution.py:72
  228.7 19.9 %gather_fusion.2 = f32[1024,896]{1,0:T(8,128)} fusion(f32[64,32,896]{2,1,0:T(8,128)} %fusion.10, s32[1024]{0:T(1024)S(1)} %bitcast.79), kind=kCustom, calls=%fused_computation.2 | custom fusion | bytes 7348224 | tf_op jit(solution)/shard_map/gather | solution.py:72
  248.5 4.6 convolution_bitcast_fusion
  253.1 0.0 copy-done.4
  253.1 0.0 copy-done.6
  253.2 2.3 convolution_bitcast_fusion.1
  255.5 0.8 copy-done.2
  256.3 2.1 fusion
  258.5 0.0 all-reduce.4.cloned.1.call-update
  258.5 0.2 reduce-scatter.2.cloned.1.call-start
  258.7 0.1 copy.22
  258.8 0.1 reshape.98
  258.9 0.1 copy.21
  259.0 0.1 dynamic-slice_bitcast_fusion
  259.1 0.1 copy.20
  259.2 0.1 reshape.70
  259.3 96.2 %all-reduce.4.cloned.1.call-done = bf16[1024,2,896]{2,0,1:T(8,128)(2,1)} async-done(((bf16[1024,2,896]{2,0,1:T(8,128)(2,1)}), bf16[1024,2,896]{2,0,1:T(8,128)(2,1)}) %all-reduce.4.cloned.1.call-update) | async-done | bytes 3670032 | tf_op jit(solution)/shard_map/psum | solution.py:77
  355.5 2.5 convert_element_type.29
  358.0 2.3 fusion.3
  360.3 12.3 %gather_fusion.3 = bf16[2048,896]{1,0:T(8,128)(2,1)} fusion(bf16[1024,896]{1,0:T(8,128)(2,1)} %fusion.3, s32[2048]{0:T(1024)S(1)} %broadcast_clamp_fusion), kind=kCustom, calls=%fused_computation.3 | custom fusion | bytes 7348224 | tf_op jit(solution)/shard_map/gather | solution.py:82
  372.6 4.2 fusion.4
  376.7 0.1 broadcast_in_dim.54
  376.9 5.2 dynamic_update_slice.7
  382.0 86.1 %all-reduce.6 = bf16[64,32,64]{2,1,0:T(8,128)(2,1)S(1)} all-reduce(f32[64,32,64]{2,1,0:T(8,128)S(1)} %dynamic_update_slice.7), channel_id=1, replica_groups=mesh['rows'=8,'hidden'=32] {'rows','hidden'}, use_global_device_ids=true, to_apply=%region_6.7 | all-reduce | flops 131072 | bytes 786432 | tf_op jit(solution)/shard_map/psum | solution.py:91
  468.1 1.1 fusion.24
  469.2 3.3 scatter_custom_fusion
  472.5 6.4 %fusion.1 = bf16[1024,1024]{1,0:T(8,128)(2,1)} fusion(f32[1025,1024]{1,0:T(8,128)} %scatter_custom_fusion, bf16[1024,896]{1,0:T(8,128)(2,1)} %fusion.3, bf16[896,1024]{1,0:T(8,128)(2,1)S(1)} %copy-done), kind=kOutput, calls=%fused_computation.9 | convolution fusion | flops 1881145344 | bytes 9961472 | tf_op jit(solution)/shard_map/dot_general | solution.py:106
  478.9 0.0 reduce-scatter.2.cloned.1.call-update
  478.9 85.7 %reduce-scatter.2.cloned.1.call-done = bf16[32,1024]{1,0:T(8,128)(2,1)} async-done(((bf16[1024,1024]{1,0:T(8,128)(2,1)}), bf16[32,1024]{1,0:T(8,128)(2,1)}) %reduce-scatter.2.cloned.1.call-update) | async-done | bytes 65552 | tf_op jit(solution)/shard_map/reduce_scatter | solution.py:104
  (20 shorter events, 0.1 us)
Async XLA Ops:
  6.5 466.0 %copy-start = (bf16[896,1024]{1,0:T(8,128)(2,1)S(1)}, bf16[896,1024]{1,0:T(8,128)(2,1)}, u32[]{:S(2)}) copy-start(bf16[896,1024]{1,0:T(8,128)(2,1)} %param.13) | copy-start | bytes 5505028
  6.5 57.5 %copy-start.5 = (bf16[2,1024,128]{2,1,0:T(8,128)(2,1)S(1)}, bf16[2,1024,128]{2,1,0:T(8,128)(2,1)}, u32[]{:S(2)}) copy-start(bf16[2,1024,128]{2,1,0:T(8,128)(2,1)} %param.14) | copy-start | bytes 1572868
  6.5 54.8 %all-gather.2.cloned.1.call-start = ((), (), s32[]{:S(2)}) async-start(), calls=%async_computation.1 | async-start | bytes 2162688 | tf_op jit(solution)/shard_map/all_gather | solution.py:50
  7.3 348.2 %all-reduce.4.cloned.1.call-start = ((), (), s32[]{:S(2)}) async-start(), calls=%async_computation.2 | async-start | bytes 7340032 | tf_op jit(solution)/shard_map/psum | solution.py:77
  199.2 5.5 copy-start.3
  248.5 4.6 copy-start.4
  248.5 4.6 copy-start.6
  253.2 2.3 copy-start.1
  253.2 3.2 copy-start.2
  258.5 306.1 %reduce-scatter.2.cloned.1.call-start = ((), (), s32[]{:S(2)}) async-start(), calls=%async_computation.3 | async-start | bytes 2162688 | tf_op jit(solution)/shard_map/reduce_scatter | solution.py:104
  360.3 12.3 %copy-start.7 = (bf16[64,8,896]{2,1,0:T(8,128)(2,1)S(1)}, bf16[64,8,896]{2,1,0:T(8,128)(2,1)}, u32[]{:S(2)}) copy-start(bf16[64,8,896]{2,1,0:T(8,128)(2,1)} %param.16) | copy-start | bytes 2752516
Sparse Core Ops, SparseCore 0:
  9.9 51.3 all-gather.1
  258.6 96.8 all-reduce.3
  479.0 85.4 reduce-scatter.1
where the time goes:
time: 572 us; the launch traced here: 571 us
  blocking collectives  217 us (38%)
  waiting for transfers between devices  210 us (37%)
  local copies, waits for them, and re-layouts  70.6 us (12%)
  other arithmetic  32.2 us (6%)
  matrix products  28.5 us (5%)
  between operations  13.3 us (2%)
    psum x1, blocking collectives, per_device(): rank_total = lax.psum(placed, ('rows', 'hidden'))  131 us
    psum x1, waiting for transfers between devices, per_device(): lax.psum((jnp.stack([gate_term, up_term], axis=1) + adapter_rows).astype(...  96.2 us
    psum x1, blocking collectives, per_device(): down_total = lax.psum(placed_down, ('rows', 'hidden'))  86.1 us
    reduce_scatter x1, waiting for transfers between devices, per_device(): lax.psum_scatter((jnp.dot(hidden_all, down_weight, preferred_element_type...  85.7 us
    gather x2, local copies, waits for them, and re-layouts, per_device(): halves.append(grouped_rows[snap_owner, slot_index])  39.7 us
    all_gather x1, waiting for transfers between devices, per_device(): gathered = lax.all_gather(tokens, 'hidden', axis=0, tiled=True)  26.9 us
    another operation x3, other arithmetic  18.2 us
    gather x1, local copies, waits for them, and re-layouts, per_device(): hidden_all[clamped_index]  12.3 us
  transfers between devices with their start and end apart: 3, of which 3 were waited for; matrix products, arithmetic and copies ran while one was open for 5% of the time, Pallas kernels for 0%

commit v1 on v0

v1 whole, which is shorter than its diff:
```python
import jax
import jax.numpy as jnp
from jax import lax
from jax.experimental import pallas as pl
from jax.experimental.pallas import tpu as pltpu
from jax.sharding import PartitionSpec as P

BF = jnp.bfloat16
F32 = jnp.float32
NX, NY, NZ = 4, 4, 8
ROWS, HID = "rows", "hidden"


def _h(x, y, c):
    return (x * NY + y) * 2 + c


def _plane(f):
    return [
        (_h(x, y, c), _h(*f(x, y, c))) for x in range(NX) for y in range(NY) for c in range(2)
    ]


def _on_x(k):
    return lambda x, y, c: ((x + k) % NX, y, c)


def _on_y(k):
    return lambda x, y, c: (x, (y + k) % NY, c)


FIRST = {k: _plane(lambda x, y, c, k=k: (_on_y(k) if c else _on_x(k))(x, y, c)) for k in (1, 2, 3)}
SECOND = {k: _plane(lambda x, y, c, k=k: (_on_x(k) if c else _on_y(k))(x, y, c)) for k in (1, 2, 3)}
SIBLING = _plane(lambda x, y, c: (x, y, 1 - c))
UP_Z = [(i, (i + 1) % NZ) for i in range(NZ)]
DOWN_Z = [(i, (i - 1) % NZ) for i in range(NZ)]


def _params(mib):
    return pltpu.CompilerParams(vmem_limit_bytes=mib << 20)


def _dot(a, b):
    return jnp.dot(a, b, preferred_element_type=F32)


def _dot_nt(a, b):
    return lax.dot_general(a, b, (((1,), (1,)), ((), ())), preferred_element_type=F32)


VM = pl.BlockSpec(memory_space=pltpu.VMEM)
ANY = pl.BlockSpec(memory_space=pl.ANY)
SM = pl.BlockSpec(memory_space=pltpu.SMEM)


def rank_kernel(pick_ref, own_ref, sib_ref, maps_ref, out_ref):
    half = own_ref.shape[0]
    picked = _dot(pick_ref[:, :half], own_ref[...]) + _dot(pick_ref[:, half:], sib_ref[...])
    picked = picked.astype(BF)
    cap = picked.shape[0] // 2
    ranks = jnp.concatenate(
        [_dot(picked[i * cap : (i + 1) * cap], maps_ref[i]) for i in range(2)], axis=0
    )
    turned = ranks.T
    blocks, k = out_ref.shape[0], out_ref.shape[1]
    side = blocks * k
    out_ref[...] = jnp.concatenate(
        [turned[:side].reshape(blocks, k, 2 * cap), turned[side:].reshape(blocks, k, 2 * cap)],
        axis=2,
    )


def up_kernel(
    place_ref, snap_ref, slot_ref, ranks_ref, own_ref, sib_ref, gate_ref, up_ref, mid_ref, out_ref,
    rows_ref, gate_v, up_v, mid_v, sems, row_sems,
):
    weights = [
        pltpu.make_async_copy(gate_ref, gate_v, sems.at[0]),
        pltpu.make_async_copy(up_ref, up_v, sems.at[1]),
        pltpu.make_async_copy(mid_ref, mid_v, sems.at[2]),
    ]
    moves = []
    for p in range(32):
        source = own_ref if p < 16 else sib_ref
        moves.append(
            pltpu.make_async_copy(
                source.at[pl.ds((p % 16) * 32, 32)],
                rows_ref.at[pl.ds(pl.multiple_of(place_ref[p] * 32, 32), 32)],
                row_sems.at[p],
            )
        )
    for copy in moves + weights:
        copy.start()
    for copy in moves + weights:
        copy.wait()
    block = 256
    ranks = ranks_ref[...]

    def body(i, carry):
        at = pl.ds(pl.multiple_of(i * block, block), block)
        rows = rows_ref[at, :]
        snap = snap_ref[at, :]
        slot = slot_ref[at, :]
        lane = lax.broadcasted_iota(jnp.int32, (block, 128), 1)
        column = lax.broadcasted_iota(jnp.int32, (block, 256), 1)
        for j in range(2):
            spread = []
            for l in range(2):
                hot = jnp.where(lane == slot + 32 * (2 * j + l), 1.0, 0.0).astype(BF)
                wide = _dot_nt(hot, ranks)
                spread.append(jnp.where(2 * (column // 8) + l == snap, wide, 0.0).astype(BF))
            total = _dot(rows, (up_v if j else gate_v)[...])
            total += _dot(jnp.concatenate(spread, axis=1), mid_v[j])
            out_ref[j, at, :] = total.astype(BF)
        return carry

    lax.fori_loop(0, rows_ref.shape[0] // block, body, 0)


def down_kernel(
    place_ref, owner_ref, snap_ref, *rest
):
    pieces = rest[:9]
    weight_ref, map_ref, out_ref, rank_ref, hid_v, weight_v, map_v, sems = rest[9:]
    copies, row = [], 0
    for n, piece in enumerate(pieces):
        copies.append(
            pltpu.make_async_copy(piece, hid_v.at[pl.ds(row, piece.shape[0])], sems.at[n])
        )
        row += piece.shape[0]
    copies.append(pltpu.make_async_copy(map_ref, map_v, sems.at[9]))
    copies.append(pltpu.make_async_copy(weight_ref, weight_v, sems.at[10]))
    for copy in copies:
        copy.start()
    for copy in copies:
        copy.wait()
    block = 256

    def body(i, carry):
        at = pl.ds(pl.multiple_of(i * block, block), block)
        hidden = hid_v[at, :]
        wide = _dot_nt(map_v[...], hidden)
        snap = snap_ref[pl.ds(i, 1), :]
        ranks = jnp.zeros((8, block), F32)
        for s in range(64):
            ranks += jnp.where(snap == s, wide[8 * s : 8 * s + 8], 0.0)
        for q in range(block // 32):
            rank_ref[owner_ref[i * (block // 32) + q]] = ranks[:, 32 * q : 32 * q + 32]
        total = _dot(hidden, weight_v[...]).astype(BF)
        for q in range(block // 32):
            to = pl.multiple_of(place_ref[i * (block // 32) + q] * 32, 32)
            out_ref[pl.ds(to, 32), :] = total[32 * q : 32 * q + 32]
        return carry

    lax.fori_loop(0, hid_v.shape[0] // block, body, 0)


def gather_rows(x):
    wave = jnp.concatenate([x] + [lax.ppermute(x, HID, FIRST[k]) for k in (1, 2, 3)], axis=0)
    wave = jnp.concatenate([wave] + [lax.ppermute(wave, HID, SECOND[k]) for k in (1, 2, 3)], axis=0)
    return wave, lax.ppermute(wave, HID, SIBLING)


def add_up(parts):
    total = parts[0].astype(F32)
    for part in parts[1:]:
        total = total + part.astype(F32)
    return total


def scatter_rows(x):
    n = x.shape[0]
    x = add_up([x[: n // 2], lax.ppermute(x[n // 2 :], HID, SIBLING)]).astype(BF)
    for wave in (FIRST, SECOND):
        n = x.shape[0] // 4
        parts = [x[:n]] + [
            lax.ppermute(x[k * n : (k + 1) * n], HID, wave[k]) for k in (1, 2, 3)
        ]
        x = add_up(parts)
        if wave is FIRST:
            x = x.astype(BF)
    return x


def reduce_z(parts):
    going = {}
    for step in range(4):
        for j in range(2):
            up_hops = 3 + j
            for sign, hops, perm in ((1, up_hops, UP_Z), (-1, 7 - up_hops, DOWN_Z)):
                hop = step - (4 - hops)
                if hop < 0:
                    continue
                term = parts[j][(sign * (hops - hop)) % NZ]
                if hop:
                    term = going[j, sign] + term
                going[j, sign] = lax.ppermute(term, ROWS, perm)
    return [add_up([going[j, 1], going[j, -1], parts[j][0]]) for j in range(2)]


def gather_z(x):
    half = x.shape[0] // 2
    ups, downs = [x], [x]
    for _ in range(3):
        ups.append(lax.ppermute(ups[-1], ROWS, UP_Z))
        downs.append(lax.ppermute(downs[-1], ROWS, DOWN_Z))
    far = [
        lax.ppermute(ups[3][:half], ROWS, UP_Z),
        lax.ppermute(downs[3][half:], ROWS, DOWN_Z),
    ]
    return [x] + downs[1:] + far + ups[:0:-1]


def per_device(
    tokens, snapshot, gate_weight, up_weight, down_weight, input_maps, middle_maps, down_in, down_out
):
    z, h = lax.axis_index(ROWS), lax.axis_index(HID)
    x, y, c = h // (2 * NY), h // 2 % NY, h % 2
    count = snapshot.shape[0]
    units = gate_weight.shape[1]
    width = tokens.shape[1]
    snaps = middle_maps.shape[0]

    owner = jnp.arange(32, dtype=jnp.int32)
    ox, oy, oc = owner // (2 * NY), owner // 2 % NY, owner % 2
    side = oc ^ c
    dx, dy = (x - ox) % NX, (y - oy) % NY
    arrives = side * 16 + jnp.where(oc == 0, dy * 4 + dx, dx * 4 + dy)
    ex, ey = (ox - x) % NX, (oy - y) % NY
    leaves = side * 16 + jnp.where(oc == 0, ex * 4 + ey, ey * 4 + ex)
    turned_owner = (owner + 4 * z) % 32
    leave_place = jnp.sum(
        jnp.where(turned_owner[:, None] == owner[None, :], leaves[None, :], 0), axis=1
    )
    turned = (owner - 4 * z) % 32
    at_position = (arrives[None, :] == owner[:, None])
    row_place = jnp.sum(jnp.where(at_position, turned[None, :], 0), axis=1)

    flat = snapshot[:, 0]
    index = jnp.arange(count, dtype=jnp.int32)
    same = (flat[:, None] == flat[None, :]) & (index[None, :] < index[:, None])
    slot = jnp.sum(same.astype(jnp.int32), axis=1)

    def turn(v):
        return lax.dynamic_slice_in_dim(jnp.concatenate([v, v]), z * (count // NZ), count)

    snap_turned, slot_turned = turn(flat), turn(slot)

    def by_arrival(v):
        v = v.reshape(1, 32, 32)
        return jnp.sum(jnp.where(at_position[:, :, None], v, 0), axis=1).reshape(count)

    key = by_arrival(flat * 32 + slot)
    pick = (key[None, :] == (64 * h + jnp.arange(64, dtype=jnp.int32))[:, None]).astype(BF)
    middle = (
        middle_maps.reshape(snaps // 2, 2, 2, 8, units)
        .transpose(2, 1, 0, 3, 4)
        .reshape(2, snaps * 8, units)
    )

    own, sib = gather_rows(tokens)
    down_out, own, sib = lax.optimization_barrier((down_out, own, sib))
    down_maps = lax.all_gather(down_out, HID, axis=0, tiled=True)

    ranks = pl.pallas_call(
        rank_kernel,
        out_shape=jax.ShapeDtypeStruct((NZ, 8, 128), F32),
        in_specs=[VM] * 4,
        out_specs=VM,
        compiler_params=_params(32),
        name="rank",
    )(pick, own, sib, input_maps)
    ranks = add_up(list(lax.all_to_all(ranks, ROWS, 0, 0))).astype(BF)
    ranks = lax.all_to_all(jnp.broadcast_to(ranks[None], (32, 8, 128)), HID, 0, 0)

    both = pl.pallas_call(
        up_kernel,
        out_shape=jax.ShapeDtypeStruct((2, count, units), BF),
        in_specs=[SM, VM, VM, VM, ANY, ANY, ANY, ANY, ANY],
        out_specs=VM,
        scratch_shapes=[
            pltpu.VMEM((count, width), BF),
            pltpu.VMEM((width, units), BF),
            pltpu.VMEM((width, units), BF),
            pltpu.VMEM((2, snaps * 8, units), BF),
            pltpu.SemaphoreType.DMA((3,)),
            pltpu.SemaphoreType.DMA((32,)),
        ],
        compiler_params=_params(48),
        name="gate_up",
    )(
        row_place, snap_turned[:, None], slot_turned[:, None], ranks.reshape(256, 128),
        own, sib, gate_weight, up_weight, middle,
    )
    both = both.reshape(2, NZ, count // NZ, units)
    gate, up = reduce_z([[both[j, i] for i in range(NZ)] for j in range(2)])
    hidden = (jax.nn.silu(gate) * up).astype(BF)
    pieces = gather_z(hidden)

    base, partial = pl.pallas_call(
        down_kernel,
        out_shape=(
            jax.ShapeDtypeStruct((count, width), BF),
            jax.ShapeDtypeStruct((32, 8, 32), F32),
        ),
        in_specs=[SM, SM, VM] + [ANY] * 11,
        out_specs=(VM, VM),
        scratch_shapes=[
            pltpu.VMEM((count, units), BF),
            pltpu.VMEM((units, width), BF),
            pltpu.VMEM((snaps * 8, units), BF),
            pltpu.SemaphoreType.DMA((11,)),
        ],
        compiler_params=_params(48),
        name="down",
    )(
        leave_place, turned_owner, snap_turned.reshape(4, 256),
        *pieces, down_weight, down_in.reshape(snaps * 8, units),
    )
    total = scatter_rows(base)
    down_rank = add_up(list(lax.all_to_all(partial, HID, 0, 0))).astype(BF)
    down_rank = lax.all_to_all(jnp.broadcast_to(down_rank[None], (NZ, 8, 32)), ROWS, 0, 0)
    mine = lax.dynamic_slice_in_dim(flat, h * 32, 32)
    spread = jnp.where(
        mine[None, None, :] == jnp.arange(snaps, dtype=jnp.int32)[:, None, None],
        down_rank.reshape(1, NZ * 8, 32),
        jnp.zeros((), BF),
    ).reshape(snaps * NZ * 8, 32)
    lifted = lax.dot_general(
        spread, down_maps.reshape(snaps * NZ * 8, width), (((0,), (0,)), ((), ())),
        preferred_element_type=F32,
    )
    return (total + lifted).astype(BF)


def solution(mesh):
    return jax.shard_map(
        per_device,
        mesh=mesh,
        in_specs=(
            P("hidden", "rows"),
            P(),
            P("rows", "hidden"),
            P("rows", "hidden"),
            P("hidden", "rows"),
            P("hidden", "rows", None),
            P(None, None, "rows", "hidden"),
            P(None, "rows", "hidden"),
            P("hidden", None, "rows"),
        ),
        out_specs=P("hidden", "rows"),
        check_vma=False,
    )
```

time: 572 us -> 227 us (0.40)
  blocking collectives: 217 us -> 0 us
  waiting for transfers between devices: 210 us -> 69.1 us
  starting transfers between devices: 0.26 us -> 74.6 us
  local copies, waits for them, and re-layouts: 70.6 us -> 23.9 us
  Pallas kernels: 0 us -> 26.5 us
  matrix products: 28.5 us -> 5.09 us
  other arithmetic: 32.2 us -> 12.5 us
    psum x2 -> x0, blocking collectives: 217 us -> none  [the longest x1 131 us: per_device(): rank_total = lax.psum(placed, ('rows', 'hidden'))]
    psum x1 -> x0, waiting for transfers between devices: 96.2 us -> none  [per_device(): lax.psum((jnp.stack([gate_term, up_term], axis=1) + adapter_rows).astype(...]
    reduce_scatter x1 -> x0, waiting for transfers between devices: 85.7 us -> none  [per_device(): lax.psum_scatter((jnp.dot(hidden_all, down_weight, preferred_element_type...]
    gather x4 -> x0, local copies, waits for them, and re-layouts: 54.7 us -> none  [the longest x2 39.7 us: per_device(): halves.append(grouped_rows[snap_owner, slot_index])]
    ppermute x0 -> x36, waiting for transfers between devices: none -> 53.2 us  [the longest x14 27 us: reduce_z(): going[j, sign] = lax.ppermute(term, ROWS, perm)]
    ppermute x0 -> x36, starting transfers between devices: none -> 48.6 us  [the longest x14 14.5 us: reduce_z(): going[j, sign] = lax.ppermute(term, ROWS, perm)]
    all_gather x1, waiting for transfers between devices: 26.9 us -> 0.01 us  [per_device(): down_maps = lax.all_gather(down_out, HID, axis=0, tiled=True)]
    pallas_call x0 -> x3, Pallas kernels: none -> 26.5 us  [the longest x1 16.6 us: per_device(): pl.pallas_call(up_kernel, out_shape=jax.ShapeDtypeStruct((2, count, units...]
  transfers between devices with their start and end apart: 3 -> 41, of which waited for: 3 -> 27; matrix products, arithmetic and copies ran while one was open for 5% -> 12% of each run, Pallas kernels for 0% -> 12%
where the time goes in v1:
time: 227 us; the launch traced here: 226 us
  starting transfers between devices  74.6 us (33%)
  waiting for transfers between devices  69.1 us (30%)
  Pallas kernels  26.5 us (12%)
  local copies, waits for them, and re-layouts  23.9 us (11%)
  between operations  13.8 us (6%)
  other arithmetic  12.5 us (6%)
  matrix products  5.09 us (2%)
    ppermute x14, waiting for transfers between devices, reduce_z(): going[j, sign] = lax.ppermute(term, ROWS, perm)  27 us
    pallas_call x1, Pallas kernels, per_device(): pl.pallas_call(up_kernel, out_shape=jax.ShapeDtypeStruct((2, count, units...  16.6 us
    ppermute x14, starting transfers between devices, reduce_z(): going[j, sign] = lax.ppermute(term, ROWS, perm)  14.5 us
    unnamed x41, local copies, waits for them, and re-layouts  13 us
    ppermute x3, waiting for transfers between devices, gather_z(): ups.append(lax.ppermute(ups[-1], ROWS, UP_Z))  13 us
    ppermute x6, starting transfers between devices, scatter_rows(): lax.ppermute(x[k * n:(k + 1) * n], HID, wave[k])  10.6 us
    ppermute x3, starting transfers between devices, gather_z(): downs.append(lax.ppermute(downs[-1], ROWS, DOWN_Z))  10 us
    pallas_call x1, Pallas kernels, per_device(): pl.pallas_call(down_kernel, out_shape=(jax.ShapeDtypeStruct((count, width...  8.5 us
  transfers between devices with their start and end apart: 41, of which 27 were waited for; matrix products, arithmetic and copies ran while one was open for 12% of the time, Pallas kernels for 12%

profile of v1, /device:TPU:2, one launch (start us, length us, event | category | flops | bytes accessed | tf_op | source)
XLA Modules:
  0.0 225.6 jit_solution(1098078259485769955)
XLA Ops:
  6.5 1.5 collective-permute-start
  8.0 2.8 %collective-permute-start.1 = (bf16[32,1024]{1,0:T(8,128)(2,1)}, bf16[32,1024]{1,0:T(8,128)(2,1)S(1)}, u32[]{:S(2)}, u32[]{:S(2)}) collective-permute-start(bf16[32,1024]{1,0:T(8,128)(2,1)} %param.9), channel_id=1, source_target_pairs={{0,16},{1,5},{2,18},{3,7},{4,20},{5,1},{6,22},{7,3},{8,24},{9,13},... | collective-permute-start | bytes 196616 | tf_op jit(solution)/shard_map/ppermute | solution.py:159
  12.2 1.8 collective-permute-done.1
  14.0 1.3 collective-permute-done.2
  16.0 2.9 %collective-permute-start.4 = (bf16[128,1024]{1,0:T(8,128)(2,1)S(1)}, bf16[128,1024]{1,0:T(8,128)(2,1)S(1)}, u32[]{:S(2)}, u32[]{:S(2)}) collective-permute-start(bf16[128,1024]{1,0:T(8,128)(2,1)S(1)} %get-tuple-element.35), channel_id=1, source_target_pairs={{0,4},{1,17},{2,6},{3,19},{4,0},{5,21},{6,2},{7,23},{8,12},{9,25},... | collective-permute-start | bytes 786440 | tf_op jit(solution)/shard_map/ppermute | solution.py:160
  18.9 1.3 collective-permute-start.5
  20.2 2.8 %collective-permute-done.3 = bf16[128,1024]{1,0:T(8,128)(2,1)S(1)} collective-permute-done((bf16[128,1024]{1,0:T(8,128)(2,1)S(1)}, bf16[128,1024]{1,0:T(8,128)(2,1)S(1)}, u32[]{:S(2)}, u32[]{:S(2)}) %collective-permute-start.3) | collective-permute-done | bytes 262176 | tf_op jit(solution)/shard_map/ppermute | solution.py:160
  23.0 3.0 %collective-permute-done.4 = bf16[128,1024]{1,0:T(8,128)(2,1)S(1)} collective-permute-done((bf16[128,1024]{1,0:T(8,128)(2,1)S(1)}, bf16[128,1024]{1,0:T(8,128)(2,1)S(1)}, u32[]{:S(2)}, u32[]{:S(2)}) %collective-permute-start.4) | collective-permute-done | bytes 262176 | tf_op jit(solution)/shard_map/ppermute | solution.py:160
  26.8 2.6 %collective-permute-done.6.sib_ref = bf16[512,1024]{1,0:T(8,128)(2,1)S(1)} collective-permute-done((bf16[512,1024]{1,0:T(8,128)(2,1)S(1)}, bf16[512,1024]{1,0:T(8,128)(2,1)S(1)}, u32[]{:S(2)}, u32[]{:S(2)}) %collective-permute-start.6) | collective-permute-done | bytes 1048608 | tf_op jit(solution)/shard_map/ppermute | solution.py:161
  29.5 1.3 convert_reduce_fusion
  33.7 3.0 %copy.20 = bf16[32,2,2,8,896]{4,3,0,1,2:T(8,128)(2,1)} copy(bf16[32,2,2,8,896]{4,3,2,1,0:T(8,128)(2,1)} %bitcast.88) | data formatting | bytes 3670016 | tf_op jit(solution)/shard_map/reshape | solution.py:256
  36.7 1.4 rank.1
  38.1 7.8 %all-to-all-start = ((f32[8,8,128]{2,1,0:T(8,128)}), f32[8,8,128]{2,1,0:T(8,128)S(1)}, u32[]{:S(2)}, u32[]{:S(2)}) async-start(f32[8,8,128]{2,1,0:T(8,128)} %rank.1), calls=%async_computation | async-start | bytes 65536 | tf_op jit(solution)/shard_map/all_to_all | solution.py:273
  46.0 8.0 %all-to-all-done = f32[8,8,128]{2,1,0:T(8,128)S(1)} async-done(((f32[8,8,128]{2,1,0:T(8,128)}), f32[8,8,128]{2,1,0:T(8,128)S(1)}, u32[]{:S(2)}, u32[]{:S(2)}) %all-to-all-start) | async-done | bytes 32800 | tf_op jit(solution)/shard_map/all_to_all | solution.py:273
  54.7 7.8 %all-to-all-start.1 = ((bf16[32,8,128]{2,1,0:T(8,128)(2,1)}), bf16[32,8,128]{2,1,0:T(8,128)(2,1)S(1)}, u32[]{:S(2)}, u32[]{:S(2)}) async-start(bf16[32,8,128]{2,1,0:T(8,128)(2,1)} %broadcast_in_dim.103), calls=%async_computation.1 | async-start | bytes 131072 | tf_op jit(solution)/shard_map/all_to_all | solution.py:274
  62.6 6.2 %all-to-all-done.1 = bf16[32,8,128]{2,1,0:T(8,128)(2,1)S(1)} async-done(((bf16[32,8,128]{2,1,0:T(8,128)(2,1)}), bf16[32,8,128]{2,1,0:T(8,128)(2,1)S(1)}, u32[]{:S(2)}, u32[]{:S(2)}) %all-to-all-start.1) | async-done | bytes 65568 | tf_op jit(solution)/shard_map/all_to_all | solution.py:274
  68.8 1.5 copy-done
  70.3 16.6 %gate_up.1 = bf16[2,1024,896]{2,1,0:T(8,128)(2,1)} custom-call(s32[32]{0:T(128)S(1)} %select_reduce_fusion.1.place_ref, s32[1024,1]{1,0:T(8,128)S(1)} %copy.21.snap_ref, s32[1024,1]{1,0:T(8,128)S(1)} %copy.22.slot_ref, bf16[256,128]{1,0:T(8,128)(2,1)S(1)} %bitcast.81, bf16[512,1024]{1,0:T(8,128)(2,1)S(1)} %constant_dynamic-update-slice_fusion.4.own_ref, ...), custom_call_target="tpu_custom_call" | custom-call | tf_op jit(solution)/shard_map/gate_up/pallas_call | solution.py:276
  86.9 1.4 slice_bitcast_fusion.15
  88.6 1.8 collective-permute-start.14
  90.4 1.5 collective-permute-start.18
  92.4 4.4 %collective-permute-done.10 = bf16[128,896]{1,0:T(8,128)(2,1)S(1)} collective-permute-done((bf16[128,896]{1,0:T(8,128)(2,1)S(1)}, bf16[128,896]{1,0:T(8,128)(2,1)S(1)}, u32[]{:S(2)}, u32[]{:S(2)}) %collective-permute-start.10) | collective-permute-done | bytes 229408 | tf_op jit(solution)/shard_map/ppermute | solution.py:197
  96.8 1.5 collective-permute-done.14
  98.3 1.1 fusion.14
  99.5 2.0 collective-permute-start.15
  101.6 1.2 collective-permute-done.7
  102.8 3.1 %collective-permute-done.11 = bf16[128,896]{1,0:T(8,128)(2,1)S(1)} collective-permute-done((bf16[128,896]{1,0:T(8,128)(2,1)S(1)}, bf16[128,896]{1,0:T(8,128)(2,1)S(1)}, u32[]{:S(2)}, u32[]{:S(2)}) %collective-permute-start.11) | collective-permute-done | bytes 229408 | tf_op jit(solution)/shard_map/ppermute | solution.py:197
  105.9 1.3 collective-permute-done.15
  107.2 1.4 fusion.16
  108.9 1.8 collective-permute-start.16
  110.7 1.4 collective-permute-start.19
  112.7 3.9 %collective-permute-done.12 = bf16[128,896]{1,0:T(8,128)(2,1)S(1)} collective-permute-done((bf16[128,896]{1,0:T(8,128)(2,1)S(1)}, bf16[128,896]{1,0:T(8,128)(2,1)S(1)}, u32[]{:S(2)}, u32[]{:S(2)}) %collective-permute-start.12) | collective-permute-done | bytes 229408 | tf_op jit(solution)/shard_map/ppermute | solution.py:197
  116.6 1.6 collective-permute-done.16
  119.1 1.6 collective-permute-done.8
  120.7 1.4 fusion.15
  122.5 1.7 collective-permute-start.17
  124.2 1.5 collective-permute-start.20
  126.2 3.3 %collective-permute-done.13 = bf16[128,896]{1,0:T(8,128)(2,1)S(1)} collective-permute-done((bf16[128,896]{1,0:T(8,128)(2,1)S(1)}, bf16[128,896]{1,0:T(8,128)(2,1)S(1)}, u32[]{:S(2)}, u32[]{:S(2)}) %collective-permute-start.13) | collective-permute-done | bytes 229408 | tf_op jit(solution)/shard_map/ppermute | solution.py:197
  129.5 1.7 collective-permute-done.17
  132.0 1.7 collective-permute-done.9
  133.7 1.3 fusion.4.rest_0_
  135.1 3.2 %collective-permute-start.21 = (bf16[128,896]{1,0:T(8,128)(2,1)S(1)}, bf16[128,896]{1,0:T(8,128)(2,1)S(1)}, u32[]{:S(2)}, u32[]{:S(2)}) collective-permute-start(bf16[128,896]{1,0:T(8,128)(2,1)S(1)} %fusion.4.rest_0_), channel_id=1, source_target_pairs={{0,224},{32,0},{64,32},{96,64},{128,96},{160,128},{192,160},{224,1... | collective-permute-start | bytes 688136 | tf_op jit(solution)/shard_map/ppermute | solution.py:206
  138.3 4.5 %collective-permute-done.24.rest_8_ = bf16[128,896]{1,0:T(8,128)(2,1)S(1)} collective-permute-done((bf16[128,896]{1,0:T(8,128)(2,1)S(1)}, bf16[128,896]{1,0:T(8,128)(2,1)S(1)}, u32[]{:S(2)}, u32[]{:S(2)}) %collective-permute-start.24) | collective-permute-done | bytes 229408 | tf_op jit(solution)/shard_map/ppermute | solution.py:205
  143.6 3.2 %collective-permute-start.22 = (bf16[128,896]{1,0:T(8,128)(2,1)S(1)}, bf16[128,896]{1,0:T(8,128)(2,1)S(1)}, u32[]{:S(2)}, u32[]{:S(2)}) collective-permute-start(bf16[128,896]{1,0:T(8,128)(2,1)S(1)} %collective-permute-done.21.rest_1_), channel_id=1, source_target_pairs={{0,224},{32,0},{64,32},{96,64},{128,96},{160,128},{192,160},{224,1... | collective-permute-start | bytes 688136 | tf_op jit(solution)/shard_map/ppermute | solution.py:206
  147.5 4.3 %collective-permute-done.25.rest_7_ = bf16[128,896]{1,0:T(8,128)(2,1)S(1)} collective-permute-done((bf16[128,896]{1,0:T(8,128)(2,1)S(1)}, bf16[128,896]{1,0:T(8,128)(2,1)S(1)}, u32[]{:S(2)}, u32[]{:S(2)}) %collective-permute-start.25) | collective-permute-done | bytes 229408 | tf_op jit(solution)/shard_map/ppermute | solution.py:205
  152.5 3.6 %collective-permute-start.23 = (bf16[128,896]{1,0:T(8,128)(2,1)S(1)}, bf16[128,896]{1,0:T(8,128)(2,1)S(1)}, u32[]{:S(2)}, u32[]{:S(2)}) collective-permute-start(bf16[128,896]{1,0:T(8,128)(2,1)S(1)} %collective-permute-done.22.rest_2_), channel_id=1, source_target_pairs={{0,224},{32,0},{64,32},{96,64},{128,96},{160,128},{192,160},{224,1... | collective-permute-start | bytes 688136 | tf_op jit(solution)/shard_map/ppermute | solution.py:206
  156.1 4.2 %collective-permute-done.26.rest_6_ = bf16[128,896]{1,0:T(8,128)(2,1)S(1)} collective-permute-done((bf16[128,896]{1,0:T(8,128)(2,1)S(1)}, bf16[128,896]{1,0:T(8,128)(2,1)S(1)}, u32[]{:S(2)}, u32[]{:S(2)}) %collective-permute-start.26) | collective-permute-done | bytes 229408 | tf_op jit(solution)/shard_map/ppermute | solution.py:205
  161.6 3.6 %collective-permute-start.28 = (bf16[64,896]{1,0:T(8,128)(2,1)}, bf16[64,896]{1,0:T(8,128)(2,1)}, u32[]{:S(2)}, u32[]{:S(2)}) collective-permute-start(bf16[64,896]{1,0:T(8,128)(2,1)} %slice.129), channel_id=1, source_target_pairs={{0,224},{32,0},{64,32},{96,64},{128,96},{160,128},{192,160},{224,1... | collective-permute-start | bytes 344072 | tf_op jit(solution)/shard_map/ppermute | solution.py:209
  165.8 1.3 reshape.224.snap_ref
  168.9 0.9 copy-done.7
  172.9 8.5 %down.1 = (bf16[1024,1024]{1,0:T(8,128)(2,1)}, f32[32,8,32]{2,1,0:T(8,128)S(1)}) custom-call(s32[32]{0:T(128)S(1)} %select_reduce_fusion.2.place_ref, s32[32]{0:T(128)S(1)} %copy-done.14, s32[4,256]{1,0:T(4,128)S(1)} %copy-done.13, bf16[128,896]{1,0:T(8,128)(2,1)S(1)} %fusion.4.rest_0_, bf16[128,896]{1,0:T(8,128)(2,1)S(1)} %copy-done.7, ...), custom_call_target="tpu_custom_call" | custom-call | tf_op jit(solution)/shard_map/down/pallas_call | solution.py:300
  182.1 1.3 slice.103
  183.5 1.6 reshape.240
  185.1 5.0 %all-to-all-start.2 = ((f32[32,1,256]{2,1,0:T(1,128)}), f32[32,1,256]{2,1,0:T(1,128)S(1)}, u32[]{:S(2)}, u32[]{:S(2)}) async-start(f32[32,1,256]{2,1,0:T(1,128)} %reshape.240), calls=%async_computation.2 | async-start | bytes 65536 | tf_op jit(solution)/shard_map/all_to_all | solution.py:321
  190.1 1.6 add_convert_fusion
  191.8 1.6 collective-permute-start.30
  194.3 2.4 %collective-permute-start.32 = (bf16[128,1024]{1,0:T(8,128)(2,1)S(1)}, bf16[128,1024]{1,0:T(8,128)(2,1)S(1)}, u32[]{:S(2)}, u32[]{:S(2)}) collective-permute-start(bf16[128,1024]{1,0:T(8,128)(2,1)S(1)} %get-tuple-element.30), channel_id=1, source_target_pairs={{0,24},{1,7},{2,26},{3,1},{4,28},{5,3},{6,30},{7,5},{8,0},{9,15},{... | collective-permute-start | bytes 786440 | tf_op jit(solution)/shard_map/ppermute | solution.py:177
  199.5 5.4 %all-to-all-start.3 = ((bf16[8,2,128]{2,1,0:T(2,128)(2,1)}), bf16[8,2,128]{2,1,0:T(2,128)(2,1)S(1)}, u32[]{:S(2)}, u32[]{:S(2)}) async-start(bf16[8,2,128]{2,1,0:T(2,128)(2,1)} %reshape.242), calls=%async_computation.3 | async-start | bytes 8192 | tf_op jit(solution)/shard_map/all_to_all | solution.py:322
  205.1 1.6 collective-permute-start.33
  206.6 2.7 %collective-permute-start.34 = (bf16[32,1024]{1,0:T(8,128)(2,1)S(1)}, bf16[32,1024]{1,0:T(8,128)(2,1)S(1)}, u32[]{:S(2)}, u32[]{:S(2)}) collective-permute-start(bf16[32,1024]{1,0:T(8,128)(2,1)S(1)} %get-tuple-element.34), channel_id=1, source_target_pairs={{0,4},{1,17},{2,6},{3,19},{4,0},{5,21},{6,2},{7,23},{8,12},{9,25},... | collective-permute-start | bytes 196616 | tf_op jit(solution)/shard_map/ppermute | solution.py:177
  209.3 1.4 collective-permute-start.35
  210.8 1.7 all-to-all-done.3
  212.6 1.0 collective-permute-done.35
  213.6 5.1 %add_convert_fusion.2 = bf16[32,1024]{1,0:T(8,128)(2,1)} fusion(bf16[32,1024]{1,0:T(8,128)(2,1)S(1)} %collective-permute-done.35, bf16[32,1024]{1,0:T(8,128)(2,1)S(1)} %collective-permute-done.34, bf16[32,1024]{1,0:T(8,128)(2,1)S(1)} %collective-permute-done.33, bf16[128,1024]{1,0:T(8,128)(2,1)S(1)} %add_convert_fusion.1, ...), kind=kOutput, calls=%fused_computation.42 | convolution fusion | flops 268861440 | bytes 8722432 | tf_op jit(solution)/shard_map/dot_general | solution.py:329
  (107 shorter events, 24.6 us)
Async XLA Ops:
  6.5 207.1 %all-gather.2.cloned.1.call-start = ((), (), s32[]{:S(2)}) async-start(), calls=%async_computation.4 | async-start | bytes 8650752 | tf_op jit(solution)/shard_map/all_gather | solution.py:263
  6.5 5.6 %collective-permute-start = (bf16[32,1024]{1,0:T(8,128)(2,1)}, bf16[32,1024]{1,0:T(8,128)(2,1)S(1)}, u32[]{:S(2)}, u32[]{:S(2)}) collective-permute-start(bf16[32,1024]{1,0:T(8,128)(2,1)} %param.9), channel_id=1, source_target_pairs={{0,8},{1,3},{2,10},{3,5},{4,12},{5,7},{6,14},{7,1},{8,16},{9,11},{... | collective-permute-start | bytes 196616 | tf_op jit(solution)/shard_map/ppermute | solution.py:159
  8.0 6.0 %collective-permute-start.1 = (bf16[32,1024]{1,0:T(8,128)(2,1)}, bf16[32,1024]{1,0:T(8,128)(2,1)S(1)}, u32[]{:S(2)}, u32[]{:S(2)}) collective-permute-start(bf16[32,1024]{1,0:T(8,128)(2,1)} %param.9), channel_id=1, source_target_pairs={{0,16},{1,5},{2,18},{3,7},{4,20},{5,1},{6,22},{7,3},{8,24},{9,13},... | collective-permute-start | bytes 196616 | tf_op jit(solution)/shard_map/ppermute | solution.py:159
  10.9 4.5 %collective-permute-start.2 = (bf16[32,1024]{1,0:T(8,128)(2,1)}, bf16[32,1024]{1,0:T(8,128)(2,1)S(1)}, u32[]{:S(2)}, u32[]{:S(2)}) collective-permute-start(bf16[32,1024]{1,0:T(8,128)(2,1)} %param.9), channel_id=1, source_target_pairs={{0,24},{1,7},{2,26},{3,1},{4,28},{5,3},{6,30},{7,5},{8,0},{9,15},{... | collective-permute-start | bytes 196616 | tf_op jit(solution)/shard_map/ppermute | solution.py:159
  15.4 7.7 %collective-permute-start.3 = (bf16[128,1024]{1,0:T(8,128)(2,1)S(1)}, bf16[128,1024]{1,0:T(8,128)(2,1)S(1)}, u32[]{:S(2)}, u32[]{:S(2)}) collective-permute-start(bf16[128,1024]{1,0:T(8,128)(2,1)S(1)} %get-tuple-element.35), channel_id=1, source_target_pairs={{0,2},{1,9},{2,4},{3,11},{4,6},{5,13},{6,0},{7,15},{8,10},{9,17},{... | collective-permute-start | bytes 786440 | tf_op jit(solution)/shard_map/ppermute | solution.py:160
  16.0 10.1 %collective-permute-start.4 = (bf16[128,1024]{1,0:T(8,128)(2,1)S(1)}, bf16[128,1024]{1,0:T(8,128)(2,1)S(1)}, u32[]{:S(2)}, u32[]{:S(2)}) collective-permute-start(bf16[128,1024]{1,0:T(8,128)(2,1)S(1)} %get-tuple-element.35), channel_id=1, source_target_pairs={{0,4},{1,17},{2,6},{3,19},{4,0},{5,21},{6,2},{7,23},{8,12},{9,25},... | collective-permute-start | bytes 786440 | tf_op jit(solution)/shard_map/ppermute | solution.py:160
  18.9 7.8 %collective-permute-start.5 = (bf16[128,1024]{1,0:T(8,128)(2,1)S(1)}, bf16[128,1024]{1,0:T(8,128)(2,1)S(1)}, u32[]{:S(2)}, u32[]{:S(2)}) collective-permute-start(bf16[128,1024]{1,0:T(8,128)(2,1)S(1)} %get-tuple-element.35), channel_id=1, source_target_pairs={{0,6},{1,25},{2,0},{3,27},{4,2},{5,29},{6,4},{7,31},{8,14},{9,1},{... | collective-permute-start | bytes 786440 | tf_op jit(solution)/shard_map/ppermute | solution.py:160
  26.7 2.7 %collective-permute-start.6 = (bf16[512,1024]{1,0:T(8,128)(2,1)S(1)}, bf16[512,1024]{1,0:T(8,128)(2,1)S(1)}, u32[]{:S(2)}, u32[]{:S(2)}) collective-permute-start(bf16[512,1024]{1,0:T(8,128)(2,1)S(1)} %constant_dynamic-update-slice_fusion.4.own_ref), channel_id=1, source_target_pairs={{0,1},{1,0},{2,3},{3,2},{4,5},{5,4},{6,7},{7,6},{8,9},{9,8},{10,11... | collective-permute-start | bytes 3145736 | tf_op jit(solution)/shard_map/ppermute | solution.py:161
  32.8 0.6 copy-start.15
  33.7 3.1 %copy-start.3 = (bf16[2,1024,128]{2,1,0:T(8,128)(2,1)S(1)}, bf16[2,1024,128]{2,1,0:T(8,128)(2,1)}, u32[]{:S(2)}) copy-start(bf16[2,1024,128]{2,1,0:T(8,128)(2,1)} %maps_ref.1) | copy-start | bytes 1572868
  38.1 15.9 %all-to-all-start = ((f32[8,8,128]{2,1,0:T(8,128)}), f32[8,8,128]{2,1,0:T(8,128)S(1)}, u32[]{:S(2)}, u32[]{:S(2)}) async-start(f32[8,8,128]{2,1,0:T(8,128)} %rank.1), calls=%async_computation | async-start | bytes 65536 | tf_op jit(solution)/shard_map/all_to_all | solution.py:273
  54.7 14.1 %all-to-all-start.1 = ((bf16[32,8,128]{2,1,0:T(8,128)(2,1)}), bf16[32,8,128]{2,1,0:T(8,128)(2,1)S(1)}, u32[]{:S(2)}, u32[]{:S(2)}) async-start(bf16[32,8,128]{2,1,0:T(8,128)(2,1)} %broadcast_in_dim.103), calls=%async_computation.1 | async-start | bytes 131072 | tf_op jit(solution)/shard_map/all_to_all | solution.py:274
  68.8 1.5 copy-start
  88.3 8.5 %collective-permute-start.10 = (bf16[128,896]{1,0:T(8,128)(2,1)S(1)}, bf16[128,896]{1,0:T(8,128)(2,1)S(1)}, u32[]{:S(2)}, u32[]{:S(2)}) collective-permute-start(bf16[128,896]{1,0:T(8,128)(2,1)S(1)} %get-tuple-element.26), channel_id=1, source_target_pairs={{0,224},{32,0},{64,32},{96,64},{128,96},{160,128},{192,160},{224,1... | collective-permute-start | bytes 688136 | tf_op jit(solution)/shard_map/ppermute | solution.py:197
  88.6 9.7 %collective-permute-start.14 = (bf16[128,896]{1,0:T(8,128)(2,1)S(1)}, bf16[128,896]{1,0:T(8,128)(2,1)S(1)}, u32[]{:S(2)}, u32[]{:S(2)}) collective-permute-start(bf16[128,896]{1,0:T(8,128)(2,1)S(1)} %get-tuple-element.25), channel_id=1, source_target_pairs={{0,32},{32,64},{64,96},{96,128},{128,160},{160,192},{192,224},{224... | collective-permute-start | bytes 688136 | tf_op jit(solution)/shard_map/ppermute | solution.py:197
  90.4 11.2 %collective-permute-start.18 = (bf16[128,896]{1,0:T(8,128)(2,1)S(1)}, bf16[128,896]{1,0:T(8,128)(2,1)S(1)}, u32[]{:S(2)}, u32[]{:S(2)}) collective-permute-start(bf16[128,896]{1,0:T(8,128)(2,1)S(1)} %get-tuple-element.24), channel_id=1, source_target_pairs={{0,224},{32,0},{64,32},{96,64},{128,96},{160,128},{192,160},{224,1... | collective-permute-start | bytes 688136 | tf_op jit(solution)/shard_map/ppermute | solution.py:197
  91.8 11.0 %collective-permute-start.7 = (bf16[128,896]{1,0:T(8,128)(2,1)S(1)}, bf16[128,896]{1,0:T(8,128)(2,1)S(1)}, u32[]{:S(2)}, u32[]{:S(2)}) collective-permute-start(bf16[128,896]{1,0:T(8,128)(2,1)S(1)} %get-tuple-element.23), channel_id=1, source_target_pairs={{0,32},{32,64},{64,96},{96,128},{128,160},{160,192},{192,224},{224... | collective-permute-start | bytes 688136 | tf_op jit(solution)/shard_map/ppermute | solution.py:197
  99.4 6.5 %collective-permute-start.11 = (bf16[128,896]{1,0:T(8,128)(2,1)S(1)}, bf16[128,896]{1,0:T(8,128)(2,1)S(1)}, u32[]{:S(2)}, u32[]{:S(2)}) collective-permute-start(bf16[128,896]{1,0:T(8,128)(2,1)S(1)} %get-tuple-element.27), channel_id=1, source_target_pairs={{0,224},{32,0},{64,32},{96,64},{128,96},{160,128},{192,160},{224,1... | collective-permute-start | bytes 688136 | tf_op jit(solution)/shard_map/ppermute | solution.py:197
  99.5 68.4 %copy-start.1 = (bf16[896,1024]{1,0:T(8,128)(2,1)S(1)}, bf16[896,1024]{1,0:T(8,128)(2,1)}, u32[]{:S(2)}) copy-start(bf16[896,1024]{1,0:T(8,128)(2,1)} %rest_9_.1) | copy-start | bytes 5505028
  99.5 68.4 %copy-start.2 = (bf16[64,8,896]{2,1,0:T(8,128)(2,1)S(1)}, bf16[64,8,896]{2,1,0:T(8,128)(2,1)}, u32[]{:S(2)}) copy-start(bf16[64,8,896]{2,1,0:T(8,128)(2,1)} %param.16) | copy-start | bytes 2752516
  99.5 7.7 %collective-permute-start.15 = (bf16[128,896]{1,0:T(8,128)(2,1)S(1)}, bf16[128,896]{1,0:T(8,128)(2,1)S(1)}, u32[]{:S(2)}, u32[]{:S(2)}) collective-permute-start(bf16[128,896]{1,0:T(8,128)(2,1)S(1)} %get-tuple-element.28), channel_id=1, source_target_pairs={{0,32},{32,64},{64,96},{96,128},{128,160},{160,192},{192,224},{224... | collective-permute-start | bytes 688136 | tf_op jit(solution)/shard_map/ppermute | solution.py:197
  108.6 8.0 %collective-permute-start.12 = (bf16[128,896]{1,0:T(8,128)(2,1)S(1)}, bf16[128,896]{1,0:T(8,128)(2,1)S(1)}, u32[]{:S(2)}, u32[]{:S(2)}) collective-permute-start(bf16[128,896]{1,0:T(8,128)(2,1)S(1)} %get-tuple-element.22), channel_id=1, source_target_pairs={{0,224},{32,0},{64,32},{96,64},{128,96},{160,128},{192,160},{224,1... | collective-permute-start | bytes 688136 | tf_op jit(solution)/shard_map/ppermute | solution.py:197
  108.9 9.4 %collective-permute-start.16 = (bf16[128,896]{1,0:T(8,128)(2,1)S(1)}, bf16[128,896]{1,0:T(8,128)(2,1)S(1)}, u32[]{:S(2)}, u32[]{:S(2)}) collective-permute-start(bf16[128,896]{1,0:T(8,128)(2,1)S(1)} %get-tuple-element.21), channel_id=1, source_target_pairs={{0,32},{32,64},{64,96},{96,128},{128,160},{160,192},{192,224},{224... | collective-permute-start | bytes 688136 | tf_op jit(solution)/shard_map/ppermute | solution.py:197
  110.7 8.4 %collective-permute-start.19 = (bf16[128,896]{1,0:T(8,128)(2,1)S(1)}, bf16[128,896]{1,0:T(8,128)(2,1)S(1)}, u32[]{:S(2)}, u32[]{:S(2)}) collective-permute-start(bf16[128,896]{1,0:T(8,128)(2,1)S(1)} %get-tuple-element.20), channel_id=1, source_target_pairs={{0,224},{32,0},{64,32},{96,64},{128,96},{160,128},{192,160},{224,1... | collective-permute-start | bytes 688136 | tf_op jit(solution)/shard_map/ppermute | solution.py:197
  112.1 8.6 %collective-permute-start.8 = (bf16[128,896]{1,0:T(8,128)(2,1)S(1)}, bf16[128,896]{1,0:T(8,128)(2,1)S(1)}, u32[]{:S(2)}, u32[]{:S(2)}) collective-permute-start(bf16[128,896]{1,0:T(8,128)(2,1)S(1)} %get-tuple-element.19), channel_id=1, source_target_pairs={{0,32},{32,64},{64,96},{96,128},{128,160},{160,192},{192,224},{224... | collective-permute-start | bytes 688136 | tf_op jit(solution)/shard_map/ppermute | solution.py:197
  122.1 7.4 %collective-permute-start.13 = (bf16[128,896]{1,0:T(8,128)(2,1)S(1)}, bf16[128,896]{1,0:T(8,128)(2,1)S(1)}, u32[]{:S(2)}, u32[]{:S(2)}) collective-permute-start(bf16[128,896]{1,0:T(8,128)(2,1)S(1)} %get-tuple-element.18), channel_id=1, source_target_pairs={{0,224},{32,0},{64,32},{96,64},{128,96},{160,128},{192,160},{224,1... | collective-permute-start | bytes 688136 | tf_op jit(solution)/shard_map/ppermute | solution.py:197
  122.5 8.8 %collective-permute-start.17 = (bf16[128,896]{1,0:T(8,128)(2,1)S(1)}, bf16[128,896]{1,0:T(8,128)(2,1)S(1)}, u32[]{:S(2)}, u32[]{:S(2)}) collective-permute-start(bf16[128,896]{1,0:T(8,128)(2,1)S(1)} %get-tuple-element.17), channel_id=1, source_target_pairs={{0,32},{32,64},{64,96},{96,128},{128,160},{160,192},{192,224},{224... | collective-permute-start | bytes 688136 | tf_op jit(solution)/shard_map/ppermute | solution.py:197
  124.2 7.8 %collective-permute-start.20 = (bf16[128,896]{1,0:T(8,128)(2,1)S(1)}, bf16[128,896]{1,0:T(8,128)(2,1)S(1)}, u32[]{:S(2)}, u32[]{:S(2)}) collective-permute-start(bf16[128,896]{1,0:T(8,128)(2,1)S(1)} %get-tuple-element.16), channel_id=1, source_target_pairs={{0,224},{32,0},{64,32},{96,64},{128,96},{160,128},{192,160},{224,1... | collective-permute-start | bytes 688136 | tf_op jit(solution)/shard_map/ppermute | solution.py:197
  125.7 8.0 %collective-permute-start.9 = (bf16[128,896]{1,0:T(8,128)(2,1)S(1)}, bf16[128,896]{1,0:T(8,128)(2,1)S(1)}, u32[]{:S(2)}, u32[]{:S(2)}) collective-permute-start(bf16[128,896]{1,0:T(8,128)(2,1)S(1)} %get-tuple-element.15), channel_id=1, source_target_pairs={{0,32},{32,64},{64,96},{96,128},{128,160},{160,192},{192,224},{224... | collective-permute-start | bytes 688136 | tf_op jit(solution)/shard_map/ppermute | solution.py:197
  135.0 7.8 %collective-permute-start.24 = (bf16[128,896]{1,0:T(8,128)(2,1)S(1)}, bf16[128,896]{1,0:T(8,128)(2,1)S(1)}, u32[]{:S(2)}, u32[]{:S(2)}) collective-permute-start(bf16[128,896]{1,0:T(8,128)(2,1)S(1)} %fusion.4.rest_0_), channel_id=1, source_target_pairs={{0,32},{32,64},{64,96},{96,128},{128,160},{160,192},{192,224},{224... | collective-permute-start | bytes 688136 | tf_op jit(solution)/shard_map/ppermute | solution.py:205
  135.1 8.4 %collective-permute-start.21 = (bf16[128,896]{1,0:T(8,128)(2,1)S(1)}, bf16[128,896]{1,0:T(8,128)(2,1)S(1)}, u32[]{:S(2)}, u32[]{:S(2)}) collective-permute-start(bf16[128,896]{1,0:T(8,128)(2,1)S(1)} %fusion.4.rest_0_), channel_id=1, source_target_pairs={{0,224},{32,0},{64,32},{96,64},{128,96},{160,128},{192,160},{224,1... | collective-permute-start | bytes 688136 | tf_op jit(solution)/shard_map/ppermute | solution.py:206
  142.8 8.9 %collective-permute-start.25 = (bf16[128,896]{1,0:T(8,128)(2,1)S(1)}, bf16[128,896]{1,0:T(8,128)(2,1)S(1)}, u32[]{:S(2)}, u32[]{:S(2)}) collective-permute-start(bf16[128,896]{1,0:T(8,128)(2,1)S(1)} %collective-permute-done.24.rest_8_), channel_id=1, source_target_pairs={{0,32},{32,64},{64,96},{96,128},{128,160},{160,192},{192,224},{224... | collective-permute-start | bytes 688136 | tf_op jit(solution)/shard_map/ppermute | solution.py:205
  142.8 0.7 copy-start.4
  143.6 8.9 %collective-permute-start.22 = (bf16[128,896]{1,0:T(8,128)(2,1)S(1)}, bf16[128,896]{1,0:T(8,128)(2,1)S(1)}, u32[]{:S(2)}, u32[]{:S(2)}) collective-permute-start(bf16[128,896]{1,0:T(8,128)(2,1)S(1)} %collective-permute-done.21.rest_1_), channel_id=1, source_target_pairs={{0,224},{32,0},{64,32},{96,64},{128,96},{160,128},{192,160},{224,1... | collective-permute-start | bytes 688136 | tf_op jit(solution)/shard_map/ppermute | solution.py:206
  146.8 0.7 copy-start.6
  151.8 8.5 %collective-permute-start.26 = (bf16[128,896]{1,0:T(8,128)(2,1)S(1)}, bf16[128,896]{1,0:T(8,128)(2,1)S(1)}, u32[]{:S(2)}, u32[]{:S(2)}) collective-permute-start(bf16[128,896]{1,0:T(8,128)(2,1)S(1)} %collective-permute-done.25.rest_7_), channel_id=1, source_target_pairs={{0,32},{32,64},{64,96},{96,128},{128,160},{160,192},{192,224},{224... | collective-permute-start | bytes 688136 | tf_op jit(solution)/shard_map/ppermute | solution.py:205
  151.8 0.7 copy-start.8
  152.5 8.4 %copy-start.10 = (bf16[128,896]{1,0:T(8,128)(2,1)}, bf16[128,896]{1,0:T(8,128)(2,1)S(1)}, u32[]{:S(2)}) copy-start(bf16[128,896]{1,0:T(8,128)(2,1)S(1)} %collective-permute-done.22.rest_2_) | copy-start | bytes 688132
  152.5 8.4 %collective-permute-start.23 = (bf16[128,896]{1,0:T(8,128)(2,1)S(1)}, bf16[128,896]{1,0:T(8,128)(2,1)S(1)}, u32[]{:S(2)}, u32[]{:S(2)}) collective-permute-start(bf16[128,896]{1,0:T(8,128)(2,1)S(1)} %collective-permute-done.22.rest_2_), channel_id=1, source_target_pairs={{0,224},{32,0},{64,32},{96,64},{128,96},{160,128},{192,160},{224,1... | collective-permute-start | bytes 688136 | tf_op jit(solution)/shard_map/ppermute | solution.py:206
  160.9 7.0 %collective-permute-start.27 = (bf16[64,896]{1,0:T(8,128)(2,1)}, bf16[64,896]{1,0:T(8,128)(2,1)S(1)}, u32[]{:S(2)}, u32[]{:S(2)}) collective-permute-start(bf16[64,896]{1,0:T(8,128)(2,1)} %slice.128), channel_id=1, source_target_pairs={{0,32},{32,64},{64,96},{96,128},{128,160},{160,192},{192,224},{224... | collective-permute-start | bytes 344072 | tf_op jit(solution)/shard_map/ppermute | solution.py:208
  161.6 6.3 %collective-permute-start.28 = (bf16[64,896]{1,0:T(8,128)(2,1)}, bf16[64,896]{1,0:T(8,128)(2,1)}, u32[]{:S(2)}, u32[]{:S(2)}) collective-permute-start(bf16[64,896]{1,0:T(8,128)(2,1)} %slice.129), channel_id=1, source_target_pairs={{0,224},{32,0},{64,32},{96,64},{128,96},{160,128},{192,160},{224,1... | collective-permute-start | bytes 344072 | tf_op jit(solution)/shard_map/ppermute | solution.py:209
  167.9 0.9 copy-start.5
  168.9 0.9 copy-start.7
  169.8 0.9 copy-start.9
  170.7 0.9 copy-start.11
  171.7 0.7 copy-start.13
  172.4 0.6 copy-start.14
  181.4 0.6 copy-start.12
  183.4 6.7 %collective-permute-start.29 = (bf16[512,1024]{1,0:T(8,128)(2,1)S(1)}, bf16[512,1024]{1,0:T(8,128)(2,1)S(1)}, u32[]{:S(2)}, u32[]{:S(2)}) collective-permute-start(bf16[512,1024]{1,0:T(8,128)(2,1)S(1)} %slice.103), channel_id=1, source_target_pairs={{0,1},{1,0},{2,3},{3,2},{4,5},{5,4},{6,7},{7,6},{8,9},{9,8},{10,11... | collective-permute-start | bytes 3145736 | tf_op jit(solution)/shard_map/ppermute | solution.py:173
  185.1 12.3 %all-to-all-start.2 = ((f32[32,1,256]{2,1,0:T(1,128)}), f32[32,1,256]{2,1,0:T(1,128)S(1)}, u32[]{:S(2)}, u32[]{:S(2)}) async-start(f32[32,1,256]{2,1,0:T(1,128)} %reshape.240), calls=%async_computation.2 | async-start | bytes 65536 | tf_op jit(solution)/shard_map/all_to_all | solution.py:321
  191.8 13.0 %collective-permute-start.30 = (bf16[128,1024]{1,0:T(8,128)(2,1)S(1)}, bf16[128,1024]{1,0:T(8,128)(2,1)S(1)}, u32[]{:S(2)}, u32[]{:S(2)}) collective-permute-start(bf16[128,1024]{1,0:T(8,128)(2,1)S(1)} %get-tuple-element.29), channel_id=1, source_target_pairs={{0,8},{1,3},{2,10},{3,5},{4,12},{5,7},{6,14},{7,1},{8,16},{9,11},{... | collective-permute-start | bytes 786440 | tf_op jit(solution)/shard_map/ppermute | solution.py:177
  193.4 11.4 %collective-permute-start.31 = (bf16[128,1024]{1,0:T(8,128)(2,1)S(1)}, bf16[128,1024]{1,0:T(8,128)(2,1)S(1)}, u32[]{:S(2)}, u32[]{:S(2)}) collective-permute-start(bf16[128,1024]{1,0:T(8,128)(2,1)S(1)} %get-tuple-element.31), channel_id=1, source_target_pairs={{0,16},{1,5},{2,18},{3,7},{4,20},{5,1},{6,22},{7,3},{8,24},{9,13},... | collective-permute-start | bytes 786440 | tf_op jit(solution)/shard_map/ppermute | solution.py:177
  194.3 10.6 %collective-permute-start.32 = (bf16[128,1024]{1,0:T(8,128)(2,1)S(1)}, bf16[128,1024]{1,0:T(8,128)(2,1)S(1)}, u32[]{:S(2)}, u32[]{:S(2)}) collective-permute-start(bf16[128,1024]{1,0:T(8,128)(2,1)S(1)} %get-tuple-element.30), channel_id=1, source_target_pairs={{0,24},{1,7},{2,26},{3,1},{4,28},{5,3},{6,30},{7,5},{8,0},{9,15},{... | collective-permute-start | bytes 786440 | tf_op jit(solution)/shard_map/ppermute | solution.py:177
  199.5 13.0 %all-to-all-start.3 = ((bf16[8,2,128]{2,1,0:T(2,128)(2,1)}), bf16[8,2,128]{2,1,0:T(2,128)(2,1)S(1)}, u32[]{:S(2)}, u32[]{:S(2)}) async-start(bf16[8,2,128]{2,1,0:T(2,128)(2,1)} %reshape.242), calls=%async_computation.3 | async-start | bytes 8192 | tf_op jit(solution)/shard_map/all_to_all | solution.py:322
  205.1 7.5 %collective-permute-start.33 = (bf16[32,1024]{1,0:T(8,128)(2,1)S(1)}, bf16[32,1024]{1,0:T(8,128)(2,1)S(1)}, u32[]{:S(2)}, u32[]{:S(2)}) collective-permute-start(bf16[32,1024]{1,0:T(8,128)(2,1)S(1)} %get-tuple-element.32), channel_id=1, source_target_pairs={{0,2},{1,9},{2,4},{3,11},{4,6},{5,13},{6,0},{7,15},{8,10},{9,17},{... | collective-permute-start | bytes 196616 | tf_op jit(solution)/shard_map/ppermute | solution.py:177
  206.6 6.0 %collective-permute-start.34 = (bf16[32,1024]{1,0:T(8,128)(2,1)S(1)}, bf16[32,1024]{1,0:T(8,128)(2,1)S(1)}, u32[]{:S(2)}, u32[]{:S(2)}) collective-permute-start(bf16[32,1024]{1,0:T(8,128)(2,1)S(1)} %get-tuple-element.34), channel_id=1, source_target_pairs={{0,4},{1,17},{2,6},{3,19},{4,0},{5,21},{6,2},{7,23},{8,12},{9,25},... | collective-permute-start | bytes 196616 | tf_op jit(solution)/shard_map/ppermute | solution.py:177
  209.3 4.3 %collective-permute-start.35 = (bf16[32,1024]{1,0:T(8,128)(2,1)S(1)}, bf16[32,1024]{1,0:T(8,128)(2,1)S(1)}, u32[]{:S(2)}, u32[]{:S(2)}) collective-permute-start(bf16[32,1024]{1,0:T(8,128)(2,1)S(1)} %get-tuple-element.33), channel_id=1, source_target_pairs={{0,6},{1,25},{2,0},{3,27},{4,2},{5,29},{6,4},{7,31},{8,14},{9,1},{... | collective-permute-start | bytes 196616 | tf_op jit(solution)/shard_map/ppermute | solution.py:177
Sparse Core Ops, SparseCore 0:
  29.6 60.3 all-gather.1
